TPU v7x, 32 devices: a whole 2x2x4 slice. The times are simulated.
32 devices in a mesh: blk: 4 (over y, core), grp: 8 (over z, x).
Axes of the slice: x: 2, y: 2, z: 4, core: 2. Of those that a mesh axis runs over, the one named last changes fastest.
Arguments:
- picture_vectors_raw: bfloat16 [4096, 1152], P(('blk', 'grp')), may hold values from -0.1875 to 0.1875
- caption_vectors_raw: bfloat16 [4096, 1152], P(('blk', 'grp')), may hold values from -0.1875 to 0.1875
- logit_multiplier: float32 [1], replicated, may hold values from 60 to 120
- offset_term: float32 [1], replicated, may hold values from -3 to -1
- incoming_adjoint: float32 [1], replicated, may hold values from 100 to 300
Outputs:
- image_grad: float32 [4096, 1152], P(('blk', 'grp'))
- text_grad: float32 [4096, 1152], P(('blk', 'grp'))
All inputs are finite; a program needn't handle non-finite values.
Results may differ from a plain program's by a relative error of at most 0.0079.
The roundings to bfloat16 on the way count: a program that leaves them out, or rounds other values in their place, can miss the bound.
Values may be sent and summed in bfloat16 or wider, within the bound.
A program may use at most 128 MiB of HBM per device.

v0:
```python
import math

import jax
import jax.numpy as jnp
from jax import lax
from jax.sharding import PartitionSpec as P


def passed_along(value, axis, steps):
    count = lax.axis_size(axis)
    pairs = [(source, (source + steps) % count) for source in range(count)]
    return lax.ppermute(value, axis, pairs)


def unit_rows(embedding):
    values = embedding.astype(jnp.float32)
    row_scale = lax.rsqrt(jnp.mean(values * values, axis=1, keepdims=True) + 1e-06) / math.sqrt(
        values.shape[1]
    )
    return (values * row_scale, row_scale)


def unit_grad(unit_vals, row_scale, upstream_grad):
    return row_scale * (
        upstream_grad - unit_vals * jnp.sum(unit_vals * upstream_grad, axis=1, keepdims=True)
    )


def assemble_interaction(
    first_operand_lines,
    second_operand_lines,
    source_position,
    target_position,
    logit_multiplier,
    offset_term,
):
    similarity_energies = lax.dot_general(
        first_operand_lines,
        second_operand_lines,
        (((1,), (1,)), ((), ())),
        preferred_element_type=jnp.float32,
    )
    similarity_matrix = logit_multiplier[0] * similarity_energies + offset_term[0]
    diag_mask = (source_position[:, None] == target_position[None, :]).astype(jnp.float32)
    return (jax.nn.sigmoid(similarity_matrix) - diag_mask).astype(jnp.bfloat16)


def column_term(all_tiles, all_rows):
    return lax.dot_general(
        all_tiles, all_rows, (((0,), (0,)), ((), ())), preferred_element_type=jnp.float32
    )


def on_device(
    picture_vectors_raw, caption_vectors_raw, logit_multiplier, offset_term, incoming_adjoint
):
    local_vectors = picture_vectors_raw.shape[0]
    embed_width = picture_vectors_raw.shape[1]
    cluster_length = lax.axis_size("grp")
    number_tiles = lax.axis_size("blk")
    block_index = lax.axis_index("blk")
    group_index = lax.axis_index("grp")
    image_unit, image_scale = unit_rows(picture_vectors_raw)
    text_unit, text_scale = unit_rows(caption_vectors_raw)
    image_half = image_unit.astype(jnp.bfloat16)
    text_half = text_unit.astype(jnp.bfloat16)
    derivative_multiplier = (
        incoming_adjoint[0] * logit_multiplier[0] / (local_vectors * cluster_length * number_tiles)
    )
    moving = (image_half, image_unit, image_scale)
    staying = (text_half, text_unit, text_scale)
    lines_each_cluster = lax.all_gather(staying[0], "grp", axis=0, tiled=True)
    group_width = lines_each_cluster.shape[0]
    target_position = block_index * group_width + lax.iota(jnp.int32, group_width)
    local_index = lax.iota(jnp.int32, local_vectors)
    current_quantity = moving[0]
    carried = jnp.zeros((local_vectors, embed_width), jnp.float32)
    tile_list = []
    rows_seen = []
    for rounds in range(number_tiles):
        if rounds > 0:
            current_quantity = passed_along(current_quantity, "blk", 1)
            carried = passed_along(carried, "blk", 1)
        source = (block_index - rounds) % number_tiles
        source_position = (source * cluster_length + group_index) * local_vectors + local_index
        coupling_tile = assemble_interaction(
            current_quantity,
            lines_each_cluster,
            source_position,
            target_position,
            logit_multiplier,
            offset_term,
        )
        carried = carried + jnp.dot(
            coupling_tile, lines_each_cluster, preferred_element_type=jnp.float32
        )
        tile_list.append(coupling_tile)
        rows_seen.append(current_quantity)
    moving_total = passed_along(carried, "blk", 1)
    all_tiles = jnp.concatenate(tile_list, axis=0)
    all_rows = jnp.concatenate(rows_seen, axis=0)
    staying_total = lax.psum_scatter(
        column_term(all_tiles, all_rows), "grp", scatter_dimension=0, tiled=True
    )
    moving_grad = unit_grad(moving[1], moving[2], derivative_multiplier * moving_total)
    staying_grad = unit_grad(staying[1], staying[2], derivative_multiplier * staying_total)
    return (moving_grad, staying_grad)


def solution(mesh):
    placed = (P(("blk", "grp"), None), P(("blk", "grp"), None), P(), P(), P())
    return jax.shard_map(
        on_device,
        mesh=mesh,
        in_specs=placed,
        out_specs=(P(("blk", "grp"), None), P(("blk", "grp"), None)),
        check_vma=False,
    )
```

profile of v0, /device:TPU:0, one launch (start us, length us, event | category | flops | bytes accessed | tf_op | source)
XLA Modules:
  0.0 182.2 jit_solution(4308400885915104444)
XLA Ops:
  7.2 0.0 all-gather.2.cloned.1.call-start
  7.2 1.1 fusion.56
  8.3 1.8 fusion.45
  10.1 0.0 all-gather.2.cloned.1.call-update
  10.1 0.0 reduce-scatter.2.cloned.1.call-start
  10.2 1.1 fusion.52
  11.3 1.1 fusion.48
  12.4 0.5 collective-permute-start.1
  14.2 5.0 %collective-permute-done.1 = bf16[128,1152]{1,0:T(8,128)(2,1)S(1)} collective-permute-done((bf16[128,1152]{1,0:T(8,128)(2,1)S(1)}, bf16[128,1152]{1,0:T(8,128)(2,1)S(1)}, u32[]{:S(2)}, u32[]{:S(2)}) %collective-permute-start.1) | collective-permute-done | bytes 294944 | tf_op jit(solution)/shard_map/ppermute | solution.py:12
  19.3 0.0 collective-permute-start.3
  19.3 6.2 %collective-permute-done.3 = bf16[128,1152]{1,0:T(8,128)(2,1)} collective-permute-done((bf16[128,1152]{1,0:T(8,128)(2,1)S(1)}, bf16[128,1152]{1,0:T(8,128)(2,1)}, u32[]{:S(2)}, u32[]{:S(2)}) %collective-permute-start.3) | collective-permute-done | bytes 294944 | tf_op jit(solution)/shard_map/ppermute | solution.py:12
  25.5 0.0 collective-permute-start.5
  25.5 40.0 %all-gather.2.cloned.1.call-done = bf16[1024,1152]{1,0:T(8,128)(2,1)} async-done(((bf16[128,1152]{1,0:T(8,128)(2,1)}), bf16[1024,1152]{1,0:T(8,128)(2,1)}) %all-gather.2.cloned.1.call-update) | async-done | bytes 2359312 | tf_op jit(solution)/shard_map/all_gather | solution.py:72
  65.6 2.8 %fusion.24 = bf16[128,1024]{1,0:T(8,128)(2,1)S(1)} fusion(bf16[128,1152]{1,0:T(8,128)(2,1)S(1)} %fusion.48, bf16[1024,1152]{1,0:T(8,128)(2,1)} %all-gather.2.cloned.1.call-done, s32[1024]{0:T(1024)S(1)} %iota_add_fusion, f32[]{:T(128)} %bitcast.24, f32[]{:T(128)} %bitcast.20, s32[128]{0:T(128)S(1)} %iota_add_fusion.4), kind=kOutput, calls=%fused_computation.29 | convolution fusion | flops 303169536 | bytes 2920968 | tf_op jit(solution)/shard_map/dot_general | solution.py:37
  68.3 0.0 copy-done.5
  68.3 0.0 copy-done
  68.3 0.9 fusion.25
  69.3 0.0 copy-start.3
  69.3 2.0 %fusion.26 = bf16[128,1024]{1,0:T(8,128)(2,1)S(1)} fusion(bf16[128,1152]{1,0:T(8,128)(2,1)} %collective-permute-done.3, bf16[1024,1152]{1,0:T(8,128)(2,1)S(1)} %copy-done, s32[1024]{0:T(1024)S(1)} %iota_add_fusion, f32[]{:T(128)} %bitcast.26, f32[]{:T(128)} %bitcast.22, s32[128]{0:T(128)S(1)} %iota_add_fusion.2), kind=kOutput, calls=%fused_computation.31 | convolution fusion | flops 303169536 | bytes 2920968 | tf_op jit(solution)/shard_map/dot_general | solution.py:37
  71.3 0.0 collective-permute-done.5
  71.3 0.0 copy-start.6
  71.3 1.9 %fusion.27 = bf16[128,1024]{1,0:T(8,128)(2,1)S(1)} fusion(bf16[128,1152]{1,0:T(8,128)(2,1)} %collective-permute-done.5, bf16[1024,1152]{1,0:T(8,128)(2,1)S(1)} %copy-done, s32[1024]{0:T(1024)S(1)} %iota_add_fusion, f32[]{:T(128)} %bitcast.25, f32[]{:T(128)} %bitcast.21, s32[128]{0:T(128)S(1)} %iota_add_fusion.1), kind=kOutput, calls=%fused_computation.32 | convolution fusion | flops 303169536 | bytes 2920968 | tf_op jit(solution)/shard_map/dot_general | solution.py:37
  73.3 0.0 copy-done.3
  73.3 0.0 copy-done.6
  73.3 4.8 %fusion.28 = f32[1024,1152]{1,0:T(8,128)} fusion(bf16[128,1152]{1,0:T(8,128)(2,1)} %collective-permute-done.5, bf16[128,1152]{1,0:T(8,128)(2,1)} %collective-permute-done.3, bf16[128,1152]{1,0:T(8,128)(2,1)S(1)} %copy-done.6, bf16[128,1152]{1,0:T(8,128)(2,1)S(1)} %fusion.48, bf16[128,1024]{1,0:T(8,128)(2,1)S(1)} %fusion.27, ...), kind=kOutput, calls=%fused_computation.33 | convolution fusion | flops 1216872448 | bytes 6946816 | tf_op jit(solution)/shard_map/dot_general | solution.py:49
  78.0 0.0 reduce-scatter.2.cloned.1.call-update
  78.1 0.0 copy-start.4
  78.1 0.5 fusion.58
  78.6 0.1 collective-permute-start
  78.7 9.3 %collective-permute-done = f32[128,1152]{1,0:T(8,128)S(1)} collective-permute-done((f32[128,1152]{1,0:T(8,128)S(1)}, f32[128,1152]{1,0:T(8,128)S(1)}, u32[]{:S(2)}, u32[]{:S(2)}) %collective-permute-start) | collective-permute-done | bytes 589856 | tf_op jit(solution)/shard_map/ppermute | solution.py:12
  88.0 0.5 convolution_add_fusion
  88.5 0.1 collective-permute-start.2
  88.6 0.5 fusion.59
  89.1 8.8 %collective-permute-done.2 = f32[128,1152]{1,0:T(8,128)S(1)} collective-permute-done((f32[128,1152]{1,0:T(8,128)S(1)}, f32[128,1152]{1,0:T(8,128)S(1)}, u32[]{:S(2)}, u32[]{:S(2)}) %collective-permute-start.2) | collective-permute-done | bytes 589856 | tf_op jit(solution)/shard_map/ppermute | solution.py:12
  97.9 0.1 add.159
  97.9 0.0 copy-start.1
  97.9 0.1 collective-permute-start.4
  98.0 0.5 fusion.60
  98.5 0.0 copy-start.2
  98.5 8.8 %collective-permute-done.4 = f32[128,1152]{1,0:T(8,128)S(1)} collective-permute-done((f32[128,1152]{1,0:T(8,128)S(1)}, f32[128,1152]{1,0:T(8,128)S(1)}, u32[]{:S(2)}, u32[]{:S(2)}) %collective-permute-start.4) | collective-permute-done | bytes 589856 | tf_op jit(solution)/shard_map/ppermute | solution.py:12
  107.3 0.1 add.166
  107.4 0.1 collective-permute-start.6
  108.1 8.6 %collective-permute-done.6 = f32[128,1152]{1,0:T(8,128)S(1)} collective-permute-done((f32[128,1152]{1,0:T(8,128)S(1)}, f32[128,1152]{1,0:T(8,128)S(1)}, u32[]{:S(2)}, u32[]{:S(2)}) %collective-permute-start.6) | collective-permute-done | bytes 589856 | tf_op jit(solution)/shard_map/ppermute | solution.py:12
  116.7 0.2 fusion.49
  117.0 1.0 fusion.51
  118.0 54.0 %reduce-scatter.2.cloned.1.call-done = f32[128,1152]{1,0:T(8,128)} async-done(((f32[1024,1152]{1,0:T(8,128)}), f32[128,1152]{1,0:T(8,128)}) %reduce-scatter.2.cloned.1.call-update) | async-done | bytes 589840 | tf_op jit(solution)/shard_map/reduce_scatter | solution.py:102
  172.0 1.3 fusion.53
  173.3 2.1 %fusion.55 = f32[128,1152]{1,0:T(8,128)} fusion(bf16[128,1152]{1,0:T(8,128)(2,1)S(1)} %copy-done.2, f32[128,1152]{1,0:T(8,128)} %reduce-scatter.2.cloned.1.call-done, f32[128]{0:T(128)S(1)} %fusion.53, f32[128]{0:T(128)S(1)} %rsqrt_multiply_fusion, f32[]{:T(128)S(6)} %div.29), kind=kLoop, calls=%fused_computation.64 | loop fusion | flops 884736 | bytes 1475588 | tf_op jit(solution)/shard_map/mul | solution.py:24
  (12 shorter events, 0.1 us)
Async XLA Ops:
  7.2 58.4 %all-gather.2.cloned.1.call-start = ((), (), s32[]{:S(2)}) async-start(), calls=%async_computation.1 | async-start | bytes 2654208 | tf_op jit(solution)/shard_map/all_gather | solution.py:72
  10.1 161.9 %reduce-scatter.2.cloned.1.call-start = ((), (), s32[]{:S(2)}) async-start(), calls=%async_computation.2 | async-start | bytes 5308416 | tf_op jit(solution)/shard_map/reduce_scatter | solution.py:102
  12.4 6.9 %collective-permute-start.1 = (bf16[128,1152]{1,0:T(8,128)(2,1)S(1)}, bf16[128,1152]{1,0:T(8,128)(2,1)S(1)}, u32[]{:S(2)}, u32[]{:S(2)}) collective-permute-start(bf16[128,1152]{1,0:T(8,128)(2,1)S(1)} %fusion.48), channel_id=1, source_target_pairs={{0,8},{8,16},{16,24},{24,0},{1,9},{9,17},{17,25},{25,1},{2,10},{10... | collective-permute-start | bytes 884744 | tf_op jit(solution)/shard_map/ppermute | solution.py:12
  19.3 49.1 %copy-start.5 = (bf16[128,1152]{1,0:T(8,128)(2,1)}, bf16[128,1152]{1,0:T(8,128)(2,1)S(1)}, u32[]{:S(2)}) copy-start(bf16[128,1152]{1,0:T(8,128)(2,1)S(1)} %collective-permute-done.1) | copy-start | bytes 884740
  19.3 6.3 %collective-permute-start.3 = (bf16[128,1152]{1,0:T(8,128)(2,1)S(1)}, bf16[128,1152]{1,0:T(8,128)(2,1)}, u32[]{:S(2)}, u32[]{:S(2)}) collective-permute-start(bf16[128,1152]{1,0:T(8,128)(2,1)S(1)} %collective-permute-done.1), channel_id=1, source_target_pairs={{0,8},{8,16},{16,24},{24,0},{1,9},{9,17},{17,25},{25,1},{2,10},{10... | collective-permute-start | bytes 884744 | tf_op jit(solution)/shard_map/ppermute | solution.py:12
  25.5 45.8 %collective-permute-start.5 = (bf16[128,1152]{1,0:T(8,128)(2,1)}, bf16[128,1152]{1,0:T(8,128)(2,1)}, u32[]{:S(2)}, u32[]{:S(2)}) collective-permute-start(bf16[128,1152]{1,0:T(8,128)(2,1)} %collective-permute-done.3), channel_id=1, source_target_pairs={{0,8},{8,16},{16,24},{24,0},{1,9},{9,17},{17,25},{25,1},{2,10},{10... | collective-permute-start | bytes 884744 | tf_op jit(solution)/shard_map/ppermute | solution.py:12
  65.6 2.8 %copy-start = (bf16[1024,1152]{1,0:T(8,128)(2,1)S(1)}, bf16[1024,1152]{1,0:T(8,128)(2,1)}, u32[]{:S(2)}) copy-start(bf16[1024,1152]{1,0:T(8,128)(2,1)} %all-gather.2.cloned.1.call-done) | copy-start | bytes 7077892
  69.3 4.0 %copy-start.3 = (bf16[128,1024]{1,0:T(8,128)(2,1)}, bf16[128,1024]{1,0:T(8,128)(2,1)S(1)}, u32[]{:S(2)}) copy-start(bf16[128,1024]{1,0:T(8,128)(2,1)S(1)} %fusion.25) | copy-start | bytes 786436
  71.3 2.0 %copy-start.6 = (bf16[128,1152]{1,0:T(8,128)(2,1)S(1)}, bf16[128,1152]{1,0:T(8,128)(2,1)}, u32[]{:S(2)}) copy-start(bf16[128,1152]{1,0:T(8,128)(2,1)} %copy-done.5) | copy-start | bytes 884740
  78.1 9.9 %copy-start.4 = (bf16[128,1024]{1,0:T(8,128)(2,1)S(1)}, bf16[128,1024]{1,0:T(8,128)(2,1)}, u32[]{:S(2)}) copy-start(bf16[128,1024]{1,0:T(8,128)(2,1)} %copy-done.3) | copy-start | bytes 786436
  78.6 9.4 %collective-permute-start = (f32[128,1152]{1,0:T(8,128)S(1)}, f32[128,1152]{1,0:T(8,128)S(1)}, u32[]{:S(2)}, u32[]{:S(2)}) collective-permute-start(f32[128,1152]{1,0:T(8,128)S(1)} %fusion.58), channel_id=1, source_target_pairs={{0,8},{8,16},{16,24},{24,0},{1,9},{9,17},{17,25},{25,1},{2,10},{10... | collective-permute-start | bytes 1769480 | tf_op jit(solution)/shard_map/ppermute | solution.py:12
  88.5 9.4 %collective-permute-start.2 = (f32[128,1152]{1,0:T(8,128)S(1)}, f32[128,1152]{1,0:T(8,128)S(1)}, u32[]{:S(2)}, u32[]{:S(2)}) collective-permute-start(f32[128,1152]{1,0:T(8,128)S(1)} %convolution_add_fusion), channel_id=1, source_target_pairs={{0,8},{8,16},{16,24},{24,0},{1,9},{9,17},{17,25},{25,1},{2,10},{10... | collective-permute-start | bytes 1769480 | tf_op jit(solution)/shard_map/ppermute | solution.py:12
  97.9 18.8 %copy-start.1 = (bf16[128,1152]{1,0:T(8,128)(2,1)S(1)}, bf16[128,1152]{1,0:T(8,128)(2,1)}, u32[]{:S(2)}) copy-start(bf16[128,1152]{1,0:T(8,128)(2,1)} %param.5) | copy-start | bytes 884740
  97.9 9.4 %collective-permute-start.4 = (f32[128,1152]{1,0:T(8,128)S(1)}, f32[128,1152]{1,0:T(8,128)S(1)}, u32[]{:S(2)}, u32[]{:S(2)}) collective-permute-start(f32[128,1152]{1,0:T(8,128)S(1)} %add.159), channel_id=1, source_target_pairs={{0,8},{8,16},{16,24},{24,0},{1,9},{9,17},{17,25},{25,1},{2,10},{10... | collective-permute-start | bytes 1769480 | tf_op jit(solution)/shard_map/ppermute | solution.py:12
  98.5 73.5 %copy-start.2 = (bf16[128,1152]{1,0:T(8,128)(2,1)S(1)}, bf16[128,1152]{1,0:T(8,128)(2,1)}, u32[]{:S(2)}) copy-start(bf16[128,1152]{1,0:T(8,128)(2,1)} %param.6) | copy-start | bytes 884740
  107.4 9.4 %collective-permute-start.6 = (f32[128,1152]{1,0:T(8,128)S(1)}, f32[128,1152]{1,0:T(8,128)S(1)}, u32[]{:S(2)}, u32[]{:S(2)}) collective-permute-start(f32[128,1152]{1,0:T(8,128)S(1)} %add.166), channel_id=1, source_target_pairs={{0,8},{8,16},{16,24},{24,0},{1,9},{9,17},{17,25},{25,1},{2,10},{10... | collective-permute-start | bytes 1769480 | tf_op jit(solution)/shard_map/ppermute | solution.py:12
Sparse Core Ops, SparseCore 0:
  10.8 54.7 all-gather.1
  78.2 93.7 reduce-scatter.1
where the time goes:
time: 183 us; the launch traced here: 182 us
  waiting for transfers between devices  141 us (77%)
  between operations  16.2 us (9%)
  matrix products  14.5 us (8%)
  other arithmetic  9.92 us (5%)
    reduce_scatter x1, waiting for transfers between devices, on_device(): lax.psum_scatter(column_term(all_tiles, all_rows), 'grp', scatter_dimensi...  54 us
    ppermute x7, waiting for transfers between devices, passed_along(): return lax.ppermute(value, axis, pairs)  46.7 us
    all_gather x1, waiting for transfers between devices, on_device(): lines_each_cluster = lax.all_gather(staying[0], 'grp', axis=0, tiled=True)  40 us
    dot_general x4, matrix products, assemble_interaction(): lax.dot_general(first_operand_lines, second_operand_lines, (((1,), (1,)),...  7.62 us
    dot_general x1, matrix products, column_term(): lax.dot_general(all_tiles, all_rows, (((0,), (0,)), ((), ())), preferred_...  4.76 us
  transfers between devices with their start and end apart: 9, of which 8 were waited for; matrix products, arithmetic and copies ran while one was open for 6% of the time, Pallas kernels for 0%

commit v1 on v0

v1 whole, which is shorter than its diff:
```python
import functools
import math

import jax
import jax.numpy as jnp
from jax import lax
from jax.experimental import pallas as pl
from jax.experimental.pallas import tpu as pltpu
from jax.sharding import PartitionSpec as P

MESH = pl.DeviceIdType.MESH
CHUNKS = 2
BF16 = jnp.bfloat16
F32 = jnp.float32


def unit_rows(embedding):
    values = embedding.astype(F32)
    row_scale = lax.rsqrt(jnp.mean(values * values, axis=1, keepdims=True) + 1e-06) / math.sqrt(
        values.shape[1]
    )
    return (values * row_scale, row_scale)


def unit_grad(unit_vals, row_scale, upstream_grad):
    return row_scale * (
        upstream_grad - unit_vals * jnp.sum(unit_vals * upstream_grad, axis=1, keepdims=True)
    )


def for_tiles(count, body):
    if count == 1:
        body(0)
    else:

        @pl.loop(0, count)
        def _(step):
            body(step)


def kernel(
    far,
    pairs,
    picture_ref,
    caption_ref,
    multiplier_ref,
    offset_ref,
    adjoint_ref,
    image_grad_ref,
    text_grad_ref,
    img,
    txt,
    coup,
    d_img,
    d_txt,
    send_x,
    recv_x,
    send_z,
    recv_z,
    send_c,
    recv_c,
    send_y,
    recv_y,
    send_w,
    recv_w,
    send_sem,
    recv_sem,
):
    rows = picture_ref.shape[0]
    part = rows // CHUNKS
    blk, grp = lax.axis_index("blk"), lax.axis_index("grp")
    y, core = lax.div(blk, 2), lax.rem(blk, 2)
    h, near, x = lax.div(grp, 4), lax.rem(lax.div(grp, 2), 2), lax.rem(grp, 2)
    at_x = (blk, h * 4 + near * 2 + (1 - x))
    at_near = (blk, h * 4 + (1 - near) * 2 + x)
    at_y = ((1 - y) * 2 + core, grp)
    at_core = (y * 2 + (1 - core), grp)
    at_far = [None] + [
        (blk, lax.rem(h + d, far) * 4 + near * 2 + x) for d in range(1, far)
    ]

    barrier = pltpu.get_barrier_semaphore()
    for peer in [at_x, at_near, at_y, at_core] + at_far[1:]:
        pl.semaphore_signal(barrier, inc=1, device_id=peer, device_id_type=MESH)

    image_unit, image_scale = unit_rows(picture_ref[...])
    text_unit, text_scale = unit_rows(caption_ref[...])
    img[pl.ds(0, rows), :] = image_unit.astype(BF16)
    txt[pl.ds(0, rows), :] = text_unit.astype(BF16)
    pl.semaphore_wait(barrier, 3 + far)

    started = []

    def send(src, src_slot, dst, dst_slot, chunk, peer):
        number = len(started)
        copy = pltpu.make_async_remote_copy(
            src_ref=src.at[pl.ds(src_slot * rows + chunk * part, part), :],
            dst_ref=dst.at[pl.ds(dst_slot * rows + chunk * part, part), :],
            send_sem=send_sem.at[number],
            recv_sem=recv_sem.at[number],
            device_id=peer,
            device_id_type=MESH,
        )
        copy.start()
        started.append(copy)
        return copy

    every = range(CHUNKS)
    img_z, txt_z, img_x, txt_y = {}, {}, {}, {}
    txt_c = []
    for c in every:
        for d in range(1, far):
            img_z[d, c] = send(img, 0, img, far - d, c, at_far[d])
        txt_z[c] = send(txt, 0, txt, 1, c, at_near)
        img_x[0, c] = send(img, 0, img, far, c, at_x)
        txt_y[0, c] = send(txt, 0, txt, 2, c, at_y)
    for c in every:
        txt_c.append(send(txt, 0, txt, 4, c, at_core))
    for c in every:
        for d in range(1, far):
            img_z[d, c].wait_recv()
            img_x[d, c] = send(img, far - d, img, 2 * far - d, c, at_x)
        txt_z[c].wait_recv()
        txt_y[1, c] = send(txt, 1, txt, 3, c, at_y)
        txt_c.append(send(txt, 1, txt, 5, c, at_core))
    for dz in (0, 1):
        for c in every:
            txt_y[dz, c].wait_recv()
            txt_c.append(send(txt, 2 + dz, txt, 6 + dz, c, at_core))
    for copy in img_x.values():
        copy.wait_recv()
    for copy in txt_c:
        copy.wait_recv()

    multiplier, offset = multiplier_ref[0], offset_ref[0]
    tile = 2 * rows

    def couple(step):
        lines = pl.ds(pl.multiple_of(step * tile, tile), tile)
        energies = lax.dot_general(
            img[lines, :], txt[...], (((1,), (1,)), ((), ())), preferred_element_type=F32
        )
        scores = multiplier * energies + offset
        coup[lines, :] = (1.0 / (1.0 + jnp.exp(-scores))).astype(BF16)

    for_tiles(far, couple)
    energies = lax.dot_general(
        img[pl.ds(0, rows), :],
        txt[pl.ds(0, rows), :],
        (((1,), (1,)), ((), ())),
        preferred_element_type=F32,
    )
    scores = multiplier * energies + offset
    same = lax.broadcasted_iota(jnp.int32, (rows, rows), 0) == lax.broadcasted_iota(
        jnp.int32, (rows, rows), 1
    )
    coup[pl.ds(0, rows), pl.ds(0, rows)] = (
        1.0 / (1.0 + jnp.exp(-scores)) - jnp.where(same, 1.0, 0.0)
    ).astype(BF16)

    def image_part(first, out):
        def body(step):
            start = pl.multiple_of(step * tile, tile)
            out[pl.ds(start, tile), :] = jnp.dot(
                coup[pl.ds(first + start, tile), :], txt[...], preferred_element_type=F32
            ).astype(out.dtype)

        for_tiles(far // 2, body)

    def text_part(slot, out, out_slot):
        out[pl.ds(out_slot * rows, tile), :] = lax.dot_general(
            coup[:, pl.ds(slot * rows, tile)],
            img[...],
            (((0,), (0,)), ((), ())),
            preferred_element_type=F32,
        ).astype(out.dtype)

    grad_c, grad_x, grad_y, grad_z, grad_w = {}, {}, {}, {}, {}
    text_part(6, send_c, 2)
    for dz in (1, 0):
        for c in every:
            grad_c[2 + dz, c] = send(send_c, 2 + dz, recv_c, 2 + dz, c, at_core)
    image_part(far * rows, send_x)
    for d in list(range(1, far)) + [0]:
        for c in every:
            grad_x[d, c] = send(send_x, d, recv_x, d, c, at_x)
    text_part(2, d_txt, 2)
    for dz in (1, 0):
        for c in every:
            grad_c[2 + dz, c].wait_recv()
            mine = pl.ds((2 + dz) * rows + c * part, part)
            send_y[pl.ds(dz * rows + c * part, part), :] = (
                d_txt[mine, :] + recv_c[mine, :].astype(F32)
            ).astype(BF16)
            grad_y[dz, c] = send(send_y, dz, recv_y, dz, c, at_y)
    text_part(4, send_c, 0)
    for dz in (1, 0):
        for c in every:
            grad_c[dz, c] = send(send_c, dz, recv_c, dz, c, at_core)
    image_part(0, d_img)
    text_part(0, d_txt, 0)

    for c in every:
        for d in range(1, far):
            grad_x[d, c].wait_recv()
            mine = pl.ds(d * rows + c * part, part)
            send_z[mine, :] = (d_img[mine, :] + recv_x[mine, :].astype(F32)).astype(BF16)
            grad_z[d, c] = send(send_z, d, recv_z, far - d, c, at_far[d])
        grad_c[1, c].wait_recv()
        grad_y[1, c].wait_recv()
        mine = pl.ds(rows + c * part, part)
        here = pl.ds(c * part, part)
        send_w[here, :] = (
            d_txt[mine, :] + recv_c[mine, :].astype(F32) + recv_y[mine, :].astype(F32)
        ).astype(BF16)
        grad_w[c] = send(send_w, 0, recv_w, 0, c, at_near)

    samples = rows * pairs
    derivative = adjoint_ref[0] * multiplier / samples
    for c in every:
        here = pl.ds(c * part, part)
        grad_x[0, c].wait_recv()
        total = d_img[here, :] + recv_x[here, :].astype(F32)
        for d in range(1, far):
            grad_z[d, c].wait_recv()
            total += recv_z[pl.ds((far - d) * rows + c * part, part), :].astype(F32)
        unit, scale = unit_rows(picture_ref[here, :])
        image_grad_ref[here, :] = unit_grad(unit, scale, derivative * total)
        grad_c[0, c].wait_recv()
        grad_y[0, c].wait_recv()
        grad_w[c].wait_recv()
        total = (
            d_txt[here, :]
            + recv_c[here, :].astype(F32)
            + recv_y[here, :].astype(F32)
            + recv_w[here, :].astype(F32)
        )
        unit, scale = unit_rows(caption_ref[here, :])
        text_grad_ref[here, :] = unit_grad(unit, scale, derivative * total)
    for copy in started:
        copy.wait_send()


def on_device(far, pairs, picture, caption, multiplier, offset, adjoint):
    rows, width = picture.shape
    copies = CHUNKS * (2 * (3 * far - 2 + 1) + 14 + 2 * far)
    vmem = pl.BlockSpec(memory_space=pltpu.VMEM)
    smem = pl.BlockSpec(memory_space=pltpu.SMEM)

    def slots(count, kind=BF16):
        return pltpu.VMEM((count * rows, width), kind)

    out = jax.ShapeDtypeStruct((rows, width), F32)
    return pl.pallas_call(
        functools.partial(kernel, far, pairs),
        out_shape=(out, out),
        in_specs=[vmem, vmem, smem, smem, smem],
        out_specs=(vmem, vmem),
        scratch_shapes=[
            slots(2 * far),
            slots(8),
            pltpu.VMEM((2 * far * rows, 8 * rows), BF16),
            slots(far, F32),
            slots(4, F32),
            slots(far),
            slots(far),
            slots(far),
            slots(far),
            slots(4),
            slots(4),
            slots(2),
            slots(2),
            slots(1),
            slots(1),
            pltpu.SemaphoreType.DMA((copies,)),
            pltpu.SemaphoreType.DMA((copies,)),
        ],
        compiler_params=pltpu.CompilerParams(
            collective_id=0, has_side_effects=True, vmem_limit_bytes=52 * 1024 * 1024
        ),
    )(picture, caption, multiplier, offset, adjoint)


def solution(mesh):
    placed = (P(("blk", "grp"), None), P(("blk", "grp"), None), P(), P(), P())
    pairs = mesh.shape["blk"] * mesh.shape["grp"]
    far = mesh.shape["grp"] // 4
    return jax.shard_map(
        functools.partial(on_device, far, pairs),
        mesh=mesh,
        in_specs=placed,
        out_specs=(P(("blk", "grp"), None), P(("blk", "grp"), None)),
        check_vma=False,
    )
```

time: 183 us -> 55.2 us (0.30)
  waiting for transfers between devices: 141 us -> 0 us
  Pallas kernels: 0 us -> 48.9 us
  matrix products: 14.5 us -> 0 us
  between operations: 16.2 us -> 2.58 us
  other arithmetic: 9.92 us -> 0 us
  local copies, waits for them, and re-layouts: 0.04 us -> 3.55 us
    reduce_scatter x1 -> x0, waiting for transfers between devices: 54 us -> none  [on_device(): lax.psum_scatter(column_term(all_tiles, all_rows), 'grp', scatter_dimensi...]
    pallas_call x0 -> x1, Pallas kernels: none -> 48.9 us  [on_device(): pl.pallas_call(functools.partial(kernel, far, pairs), out_shape=(out, out...]
    ppermute x7 -> x0, waiting for transfers between devices: 46.7 us -> none  [passed_along(): return lax.ppermute(value, axis, pairs)]
    all_gather x1 -> x0, waiting for transfers between devices: 40 us -> none  [on_device(): lines_each_cluster = lax.all_gather(staying[0], 'grp', axis=0, tiled=True)]
    dot_general x9 -> x0, matrix products: 14.5 us -> none  [the longest x4 7.62 us: assemble_interaction(): lax.dot_general(first_operand_lines, second_operand_lines, (((1,), (1,)),...]
    reduce_sum x4 -> x0, other arithmetic: 3.72 us -> none  [the longest x2 2.21 us: unit_rows(): jnp.mean(values * values, axis=1, keepdims=True) + 1e-06]
    unnamed x14 -> x6, local copies, waits for them, and re-layouts: 0.04 us -> 3.55 us
    mul x2 -> x0, other arithmetic: 3.14 us -> none  [unit_grad(): row_scale * (upstream_grad - unit_vals * jnp.sum(unit_vals * upstream_gra...]
  transfers between devices with their start and end apart: 9 -> 0, of which waited for: 8 -> 0; matrix products, arithmetic and copies ran while one was open for 6% -> 0% of each run, Pallas kernels for 0% -> 0%
where the time goes in v1:
time: 55.2 us; the launch traced here: 55 us
  Pallas kernels  48.9 us (89%)
  local copies, waits for them, and re-layouts  3.55 us (6%)
  between operations  2.58 us (5%)
    pallas_call x1, Pallas kernels, on_device(): pl.pallas_call(functools.partial(kernel, far, pairs), out_shape=(out, out...  48.9 us
    unnamed x6, local copies, waits for them, and re-layouts  3.55 us

profile of v1, /device:TPU:0, one launch (start us, length us, event | category | flops | bytes accessed | tf_op | source)
XLA Modules:
  0.0 55.0 jit_solution(2342537134273172347)
XLA Ops:
  2.6 0.0 copy-start
  2.6 1.0 %copy-done = bf16[128,1152]{1,0:T(8,128)(2,1)S(1)} copy-done((bf16[128,1152]{1,0:T(8,128)(2,1)S(1)}, bf16[128,1152]{1,0:T(8,128)(2,1)}, u32[]{:S(2)}) %copy-start) | copy-done | bytes 294936
  3.5 0.0 copy-start.1
  3.5 1.0 %copy-done.1 = bf16[128,1152]{1,0:T(8,128)(2,1)S(1)} copy-done((bf16[128,1152]{1,0:T(8,128)(2,1)S(1)}, bf16[128,1152]{1,0:T(8,128)(2,1)}, u32[]{:S(2)}) %copy-start.1) | copy-done | bytes 294936
  4.5 48.9 %shard_map.68 = (f32[128,1152]{1,0:T(8,128)S(1)}, f32[128,1152]{1,0:T(8,128)S(1)}) custom-call(bf16[128,1152]{1,0:T(8,128)(2,1)S(1)} %copy-done, bf16[128,1152]{1,0:T(8,128)(2,1)S(1)} %copy-done.1, f32[1]{0:T(128)S(6)} %copy.9.multiplier_ref, f32[1]{0:T(128)S(6)} %copy.10.offset_ref, f32[1]{0:T(128)S(6)} %copy.11.adjoint_ref), custom_call_target="tpu_custom_call" | custom-call | tf_op jit(solution)/shard_map/pallas_call | solution.py:254
  53.4 0.8 %copy.12 = f32[128,1152]{1,0:T(8,128)} copy(f32[128,1152]{1,0:T(8,128)S(1)} %get-tuple-element.4) | data formatting | bytes 1179648
  54.2 0.8 %copy.13 = f32[128,1152]{1,0:T(8,128)} copy(f32[128,1152]{1,0:T(8,128)S(1)} %get-tuple-element.5) | data formatting | bytes 1179648
Async XLA Ops:
  2.6 1.0 %copy-start = (bf16[128,1152]{1,0:T(8,128)(2,1)S(1)}, bf16[128,1152]{1,0:T(8,128)(2,1)}, u32[]{:S(2)}) copy-start(bf16[128,1152]{1,0:T(8,128)(2,1)} %picture_ref.1) | copy-start | bytes 884740
  3.5 1.0 %copy-start.1 = (bf16[128,1152]{1,0:T(8,128)(2,1)S(1)}, bf16[128,1152]{1,0:T(8,128)(2,1)}, u32[]{:S(2)}) copy-start(bf16[128,1152]{1,0:T(8,128)(2,1)} %caption_ref.1) | copy-start | bytes 884740

commit v2 on v1

v2 whole, which is shorter than its diff:
```python
import functools
import math

import jax
import jax.numpy as jnp
from jax import lax
from jax.experimental import pallas as pl
from jax.experimental.pallas import tpu as pltpu
from jax.sharding import PartitionSpec as P

MESH = pl.DeviceIdType.MESH
CHUNKS = 4
BF16 = jnp.bfloat16
F32 = jnp.float32


def unit_rows(embedding):
    values = embedding.astype(F32)
    row_scale = lax.rsqrt(jnp.mean(values * values, axis=1, keepdims=True) + 1e-06) / math.sqrt(
        values.shape[1]
    )
    return (values * row_scale, row_scale)


def unit_grad(unit_vals, row_scale, upstream_grad):
    return row_scale * (
        upstream_grad - unit_vals * jnp.sum(unit_vals * upstream_grad, axis=1, keepdims=True)
    )


def for_tiles(first, end, body):
    if end - first == 1:
        body(first)
    else:

        @pl.loop(first, end)
        def _(step):
            body(step)


def kernel(
    far,
    pairs,
    picture_hbm,
    caption_hbm,
    multiplier_ref,
    offset_ref,
    adjoint_ref,
    image_grad_ref,
    text_grad_ref,
    picture_ref,
    caption_ref,
    img,
    txt,
    coup,
    d_img,
    d_txt,
    send_x,
    recv_x,
    send_z,
    recv_z,
    send_c,
    recv_c,
    send_y,
    recv_y,
    send_w,
    recv_w,
    load_sem,
    send_sem,
    recv_sem,
):
    rows = picture_ref.shape[0]
    part = rows // CHUNKS
    load_picture = pltpu.make_async_copy(picture_hbm, picture_ref, load_sem.at[0])
    load_caption = pltpu.make_async_copy(caption_hbm, caption_ref, load_sem.at[1])
    load_picture.start()
    load_caption.start()
    blk, grp = lax.axis_index("blk"), lax.axis_index("grp")
    y, core = lax.div(blk, 2), lax.rem(blk, 2)
    h, near, x = lax.div(grp, 4), lax.rem(lax.div(grp, 2), 2), lax.rem(grp, 2)
    at_x = (blk, h * 4 + near * 2 + (1 - x))
    at_near = (blk, h * 4 + (1 - near) * 2 + x)
    at_y = ((1 - y) * 2 + core, grp)
    at_core = (y * 2 + (1 - core), grp)
    at_far = [None] + [
        (blk, lax.rem(h + d, far) * 4 + near * 2 + x) for d in range(1, far)
    ]

    barrier = pltpu.get_barrier_semaphore()
    for peer in [at_x, at_near, at_y, at_core] + at_far[1:]:
        pl.semaphore_signal(barrier, inc=1, device_id=peer, device_id_type=MESH)

    load_picture.wait()
    img[pl.ds(0, rows), :] = unit_rows(picture_ref[...])[0].astype(BF16)
    load_caption.wait()
    txt[pl.ds(0, rows), :] = unit_rows(caption_ref[...])[0].astype(BF16)
    pl.semaphore_wait(barrier, 3 + far)

    started = []

    def send(src, src_slot, dst, dst_slot, chunk, peer):
        number = len(started)
        copy = pltpu.make_async_remote_copy(
            src_ref=src.at[pl.ds(src_slot * rows + chunk * part, part), :],
            dst_ref=dst.at[pl.ds(dst_slot * rows + chunk * part, part), :],
            send_sem=send_sem.at[number],
            recv_sem=recv_sem.at[number],
            device_id=peer,
            device_id_type=MESH,
        )
        copy.start()
        started.append(copy)
        return copy

    every = range(CHUNKS)
    img_z, txt_z, img_x, txt_y, txt_c = {}, {}, {}, {}, {}
    for c in every:
        for d in range(1, far):
            img_z[d, c] = send(img, 0, img, 2 * (far - d), c, at_far[d])
        txt_z[c] = send(txt, 0, txt, 4, c, at_near)
        img_x[0, c] = send(img, 0, img, 1, c, at_x)
        txt_y[0, c] = send(txt, 0, txt, 1, c, at_y)
    for c in every:
        txt_c[0, c] = send(txt, 0, txt, 2, c, at_core)

    multiplier, offset = multiplier_ref[0], offset_ref[0]
    tile = 2 * rows

    def sigmoid_tile(lines, columns):
        energies = lax.dot_general(
            img[lines, :], txt[columns, :], (((1,), (1,)), ((), ())), preferred_element_type=F32
        )
        return 1.0 / (1.0 + jnp.exp(-(multiplier * energies + offset)))

    def near_tiles():
        lines, columns = pl.ds(0, tile), pl.ds(0, 2 * tile)
        values = sigmoid_tile(lines, columns)
        same = lax.broadcasted_iota(jnp.int32, values.shape, 0) == lax.broadcasted_iota(
            jnp.int32, values.shape, 1
        )
        same = same & (lax.broadcasted_iota(jnp.int32, values.shape, 0) < rows)
        coup[lines, columns] = (values - jnp.where(same, 1.0, 0.0)).astype(BF16)

    for c in every:
        for d in range(1, far):
            img_z[d, c].wait_recv()
            img_x[d, c] = send(img, 2 * (far - d), img, 2 * (far - d) + 1, c, at_x)
        txt_z[c].wait_recv()
        txt_y[1, c] = send(txt, 4, txt, 5, c, at_y)
        txt_c[2, c] = send(txt, 4, txt, 6, c, at_core)
        if c == CHUNKS // 2:
            for e in every:
                txt_y[0, e].wait_recv()
                txt_c[1, e] = send(txt, 1, txt, 3, e, at_core)
    for c in every:
        img_x[0, c].wait_recv()
        txt_c[0, c].wait_recv()
        txt_c[1, c].wait_recv()
    near_tiles()
    for c in every:
        txt_y[1, c].wait_recv()
        txt_c[3, c] = send(txt, 5, txt, 7, c, at_core)
    for c in every:
        for d in range(1, far):
            img_x[d, c].wait_recv()
        txt_c[2, c].wait_recv()
        txt_c[3, c].wait_recv()

    def image_part(step):
        lines = pl.ds(pl.multiple_of(step * tile, tile), tile)
        total = jnp.dot(coup[lines, :], txt[...], preferred_element_type=F32)
        here = pl.ds(pl.multiple_of(step * rows, rows), rows)
        d_img[here, :] = total[:rows]
        send_x[here, :] = total[rows:].astype(BF16)

    def far_tiles(step):
        lines = pl.ds(pl.multiple_of(step * tile, tile), tile)
        coup[lines, :] = sigmoid_tile(lines, slice(None)).astype(BF16)
        image_part(step)

    def text_part(slot):
        return lax.dot_general(
            coup[:, pl.ds(slot * rows, tile)],
            img[...],
            (((0,), (0,)), ((), ())),
            preferred_element_type=F32,
        )

    grad_c, grad_x, grad_y, grad_z, grad_w = {}, {}, {}, {}, {}
    for_tiles(1, far, far_tiles)
    for c in every:
        for d in range(1, far):
            grad_x[d, c] = send(send_x, d, recv_x, d, c, at_x)
    lines, columns = pl.ds(0, tile), pl.ds(2 * tile, 2 * tile)
    coup[lines, columns] = sigmoid_tile(lines, columns).astype(BF16)
    for dz in (1, 0):
        send_c[pl.ds(2 * dz * rows, tile), :] = text_part(dz * 4 + 2).astype(BF16)
        for dy in (1, 0):
            for c in every:
                grad_c[dz, dy, c] = send(send_c, dz * 2 + dy, recv_c, dz * 2 + dy, c, at_core)
    image_part(0)
    for c in every:
        grad_x[0, c] = send(send_x, 0, recv_x, 0, c, at_x)
    for dz in (1, 0):
        d_txt[pl.ds(2 * dz * rows, tile), :] = text_part(dz * 4)
        for c in every:
            grad_c[dz, 1, c].wait_recv()
            mine = pl.ds((2 * dz + 1) * rows + c * part, part)
            send_y[pl.ds(dz * rows + c * part, part), :] = (
                d_txt[mine, :] + recv_c[mine, :].astype(F32)
            ).astype(BF16)
            grad_y[dz, c] = send(send_y, dz, recv_y, dz, c, at_y)

    for c in every:
        for d in range(1, far):
            grad_x[d, c].wait_recv()
            mine = pl.ds(d * rows + c * part, part)
            send_z[mine, :] = (d_img[mine, :] + recv_x[mine, :].astype(F32)).astype(BF16)
            grad_z[d, c] = send(send_z, d, recv_z, far - d, c, at_far[d])
        grad_c[1, 0, c].wait_recv()
        grad_y[1, c].wait_recv()
        mine = pl.ds(2 * rows + c * part, part)
        here = pl.ds(c * part, part)
        send_w[here, :] = (
            d_txt[mine, :]
            + recv_c[mine, :].astype(F32)
            + recv_y[pl.ds(rows + c * part, part), :].astype(F32)
        ).astype(BF16)
        grad_w[c] = send(send_w, 0, recv_w, 0, c, at_near)

    samples = rows * pairs
    derivative = adjoint_ref[0] * multiplier / samples
    for c in every:
        here = pl.ds(c * part, part)
        grad_x[0, c].wait_recv()
        total = d_img[here, :] + recv_x[here, :].astype(F32)
        for d in range(1, far):
            grad_z[d, c].wait_recv()
            total += recv_z[pl.ds((far - d) * rows + c * part, part), :].astype(F32)
        unit, scale = unit_rows(picture_ref[here, :])
        image_grad_ref[here, :] = unit_grad(unit, scale, derivative * total)
        grad_c[0, 0, c].wait_recv()
        grad_y[0, c].wait_recv()
        grad_w[c].wait_recv()
        total = (
            d_txt[here, :]
            + recv_c[here, :].astype(F32)
            + recv_y[here, :].astype(F32)
            + recv_w[here, :].astype(F32)
        )
        unit, scale = unit_rows(caption_ref[here, :])
        text_grad_ref[here, :] = unit_grad(unit, scale, derivative * total)
    for copy in started:
        copy.wait_send()


def on_device(far, pairs, picture, caption, multiplier, offset, adjoint):
    rows, width = picture.shape
    copies = CHUNKS * (4 * far + 12)
    vmem = pl.BlockSpec(memory_space=pltpu.VMEM)
    hbm = pl.BlockSpec(memory_space=pltpu.HBM)
    smem = pl.BlockSpec(memory_space=pltpu.SMEM)

    def slots(count, kind=BF16):
        return pltpu.VMEM((count * rows, width), kind)

    out = jax.ShapeDtypeStruct((rows, width), F32)
    return pl.pallas_call(
        functools.partial(kernel, far, pairs),
        out_shape=(out, out),
        in_specs=[hbm, hbm, smem, smem, smem],
        out_specs=(vmem, vmem),
        scratch_shapes=[
            slots(1),
            slots(1),
            slots(2 * far),
            slots(8),
            pltpu.VMEM((2 * far * rows, 8 * rows), BF16),
            slots(far, F32),
            slots(4, F32),
            slots(far),
            slots(far),
            slots(far),
            slots(far),
            slots(4),
            slots(4),
            slots(2),
            slots(2),
            slots(1),
            slots(1),
            pltpu.SemaphoreType.DMA((2,)),
            pltpu.SemaphoreType.DMA((copies,)),
            pltpu.SemaphoreType.DMA((copies,)),
        ],
        compiler_params=pltpu.CompilerParams(
            collective_id=0, has_side_effects=True, vmem_limit_bytes=63 * 1024 * 1024
        ),
    )(picture, caption, multiplier, offset, adjoint)


def solution(mesh):
    placed = (P(("blk", "grp"), None), P(("blk", "grp"), None), P(), P(), P())
    pairs = mesh.shape["blk"] * mesh.shape["grp"]
    far = mesh.shape["grp"] // 4
    return jax.shard_map(
        functools.partial(on_device, far, pairs),
        mesh=mesh,
        in_specs=placed,
        out_specs=(P(("blk", "grp"), None), P(("blk", "grp"), None)),
        check_vma=False,
    )
```

time: 55.2 us -> 53.4 us (0.967)
  Pallas kernels: 48.9 us -> 47.8 us
  local copies, waits for them, and re-layouts: 3.55 us -> 2.8 us
    pallas_call x1, Pallas kernels: 48.9 us -> 47.8 us  [on_device(): pl.pallas_call(functools.partial(kernel, far, pairs), out_shape=(out, out...]
    unnamed x6 -> x4, local copies, waits for them, and re-layouts: 3.55 us -> 2.8 us
where the time goes in v2:
time: 53.4 us; the launch traced here: 53.2 us
  Pallas kernels  47.8 us (90%)
  local copies, waits for them, and re-layouts  2.8 us (5%)
  between operations  2.58 us (5%)
    pallas_call x1, Pallas kernels, on_device(): pl.pallas_call(functools.partial(kernel, far, pairs), out_shape=(out, out...  47.8 us
    unnamed x4, local copies, waits for them, and re-layouts  2.8 us

profile of v2, /device:TPU:0, one launch (start us, length us, event | category | flops | bytes accessed | tf_op | source)
XLA Modules:
  0.0 53.2 jit_solution(1079814265961825021)
XLA Ops:
  2.6 47.8 %shard_map.68 = (f32[128,1152]{1,0:T(8,128)}, f32[128,1152]{1,0:T(8,128)}) custom-call(bf16[128,1152]{1,0:T(8,128)(2,1)} %picture_hbm.1, bf16[128,1152]{1,0:T(8,128)(2,1)} %caption_hbm.1, f32[1]{0:T(128)S(6)} %copy.9.multiplier_ref, f32[1]{0:T(128)S(6)} %copy.10.offset_ref, f32[1]{0:T(128)S(6)} %copy.11.adjoint_ref), custom_call_target="tpu_custom_call" | custom-call | tf_op jit(solution)/shard_map/pallas_call | solution.py:268
  50.4 0.0 copy-start
  50.4 2.0 %copy.12 = f32[128,1152]{1,0:T(8,128)} copy(f32[128,1152]{1,0:T(8,128)} %get-tuple-element.4) | data formatting | bytes 1179648
  52.4 0.0 copy-done
  52.4 0.8 %copy.13 = f32[128,1152]{1,0:T(8,128)} copy(f32[128,1152]{1,0:T(8,128)S(1)} %copy-done) | data formatting | bytes 1179648
Async XLA Ops:
  50.4 2.0 %copy-start = (f32[128,1152]{1,0:T(8,128)S(1)}, f32[128,1152]{1,0:T(8,128)}, u32[]{:S(2)}) copy-start(f32[128,1152]{1,0:T(8,128)} %get-tuple-element.5) | copy-start | bytes 1769476

commit v3 on v2

--- a/solution.py
+++ b/solution.py
@@ -10,6 +10,7 @@
 
 MESH = pl.DeviceIdType.MESH
 CHUNKS = 4
+AHEAD = 2
 BF16 = jnp.bfloat16
 F32 = jnp.float32
 
@@ -96,7 +97,7 @@
     txt[pl.ds(0, rows), :] = unit_rows(caption_ref[...])[0].astype(BF16)
     pl.semaphore_wait(barrier, 3 + far)
 
-    started = []
+    started = {}
 
     def send(src, src_slot, dst, dst_slot, chunk, peer):
         number = len(started)
@@ -109,15 +110,29 @@
             device_id_type=MESH,
         )
         copy.start()
-        started.append(copy)
+        started[number] = copy
         return copy
+
+    def sent(copy):
+        copy.wait_send()
+        for number in started:
+            if started[number] is copy:
+                started[number] = None
 
     every = range(CHUNKS)
     img_z, txt_z, img_x, txt_y, txt_c = {}, {}, {}, {}, {}
-    for c in every:
-        for d in range(1, far):
+
+    def start_z(c):
+        for d in range(1, far):
+            if c > 0:
+                sent(img_z[d, c - 1])
             img_z[d, c] = send(img, 0, img, 2 * (far - d), c, at_far[d])
+        if c > 0:
+            sent(txt_z[c - 1])
         txt_z[c] = send(txt, 0, txt, 4, c, at_near)
+
+    start_z(0)
+    for c in every:
         img_x[0, c] = send(img, 0, img, 1, c, at_x)
         txt_y[0, c] = send(txt, 0, txt, 1, c, at_y)
     for c in every:
@@ -142,6 +157,8 @@
         coup[lines, columns] = (values - jnp.where(same, 1.0, 0.0)).astype(BF16)
 
     for c in every:
+        if c + 1 < CHUNKS:
+            start_z(c + 1)
         for d in range(1, far):
             img_z[d, c].wait_recv()
             img_x[d, c] = send(img, 2 * (far - d), img, 2 * (far - d) + 1, c, at_x)
@@ -187,36 +204,63 @@
         )
 
     grad_c, grad_x, grad_y, grad_z, grad_w = {}, {}, {}, {}, {}
-    for_tiles(1, far, far_tiles)
-    for c in every:
-        for d in range(1, far):
+    order_x = [[(d, c) for d in range(1, far)] for c in every] + [[(0, c)] for c in every]
+    order_y = [(1, c) for c in every] + [(0, c) for c in every]
+
+    def start_x(k):
+        if k >= AHEAD:
+            for key in order_x[k - AHEAD]:
+                sent(grad_x[key])
+        for d, c in order_x[k]:
             grad_x[d, c] = send(send_x, d, recv_x, d, c, at_x)
-    lines, columns = pl.ds(0, tile), pl.ds(2 * tile, 2 * tile)
-    coup[lines, columns] = sigmoid_tile(lines, columns).astype(BF16)
-    for dz in (1, 0):
+
+    def start_y(k):
+        if k >= AHEAD:
+            sent(grad_y[order_y[k - AHEAD]])
+        dz, c = order_y[k]
+        grad_y[dz, c] = send(send_y, dz, recv_y, dz, c, at_y)
+
+    def core_part(dz):
         send_c[pl.ds(2 * dz * rows, tile), :] = text_part(dz * 4 + 2).astype(BF16)
         for dy in (1, 0):
             for c in every:
                 grad_c[dz, dy, c] = send(send_c, dz * 2 + dy, recv_c, dz * 2 + dy, c, at_core)
+
+    def own_part(dz):
+        d_txt[pl.ds(2 * dz * rows, tile), :] = text_part(dz * 4)
+
+    def y_sum(dz, c):
+        grad_c[dz, 1, c].wait_recv()
+        mine = pl.ds((2 * dz + 1) * rows + c * part, part)
+        send_y[pl.ds(dz * rows + c * part, part), :] = (
+            d_txt[mine, :] + recv_c[mine, :].astype(F32)
+        ).astype(BF16)
+
+    for_tiles(1, far, far_tiles)
+    for k in range(AHEAD):
+        start_x(k)
+    lines, columns = pl.ds(0, tile), pl.ds(2 * tile, 2 * tile)
+    coup[lines, columns] = sigmoid_tile(lines, columns).astype(BF16)
+    core_part(1)
+    own_part(1)
+    core_part(0)
+    for c in every:
+        y_sum(1, c)
+        if c < AHEAD:
+            start_y(c)
     image_part(0)
-    for c in every:
-        grad_x[0, c] = send(send_x, 0, recv_x, 0, c, at_x)
-    for dz in (1, 0):
-        d_txt[pl.ds(2 * dz * rows, tile), :] = text_part(dz * 4)
-        for c in every:
-            grad_c[dz, 1, c].wait_recv()
-            mine = pl.ds((2 * dz + 1) * rows + c * part, part)
-            send_y[pl.ds(dz * rows + c * part, part), :] = (
-                d_txt[mine, :] + recv_c[mine, :].astype(F32)
-            ).astype(BF16)
-            grad_y[dz, c] = send(send_y, dz, recv_y, dz, c, at_y)
-
-    for c in every:
+    own_part(0)
+    for c in every:
+        y_sum(0, c)
+
+    for c in every:
+        start_x(c + AHEAD)
         for d in range(1, far):
             grad_x[d, c].wait_recv()
             mine = pl.ds(d * rows + c * part, part)
             send_z[mine, :] = (d_img[mine, :] + recv_x[mine, :].astype(F32)).astype(BF16)
             grad_z[d, c] = send(send_z, d, recv_z, far - d, c, at_far[d])
+        start_y(c + AHEAD)
         grad_c[1, 0, c].wait_recv()
         grad_y[1, c].wait_recv()
         mine = pl.ds(2 * rows + c * part, part)
@@ -227,6 +271,9 @@
             + recv_y[pl.ds(rows + c * part, part), :].astype(F32)
         ).astype(BF16)
         grad_w[c] = send(send_w, 0, recv_w, 0, c, at_near)
+    for k in range(CHUNKS + AHEAD, 2 * CHUNKS):
+        start_x(k)
+        start_y(k)
 
     samples = rows * pairs
     derivative = adjoint_ref[0] * multiplier / samples
@@ -250,8 +297,9 @@
         )
         unit, scale = unit_rows(caption_ref[here, :])
         text_grad_ref[here, :] = unit_grad(unit, scale, derivative * total)
-    for copy in started:
-        copy.wait_send()
+    for copy in started.values():
+        if copy is not None:
+            copy.wait_send()
 
 
 def on_device(far, pairs, picture, caption, multiplier, offset, adjoint):
@@ -293,7 +341,7 @@
             pltpu.SemaphoreType.DMA((copies,)),
         ],
         compiler_params=pltpu.CompilerParams(
-            collective_id=0, has_side_effects=True, vmem_limit_bytes=63 * 1024 * 1024
+            collective_id=0, has_side_effects=True, vmem_limit_bytes=52 * 1024 * 1024
         ),
     )(picture, caption, multiplier, offset, adjoint)
 

time: 53.4 us -> 52.5 us (0.983)
  Pallas kernels: 47.8 us -> 46.1 us
  local copies, waits for them, and re-layouts: 2.8 us -> 3.55 us
    pallas_call x1, Pallas kernels: 47.8 us -> 46.1 us  [on_device(): pl.pallas_call(functools.partial(kernel, far, pairs), out_shape=(out, out...]
    unnamed x4 -> x6, local copies, waits for them, and re-layouts: 2.8 us -> 3.55 us
where the time goes in v3:
time: 52.5 us; the launch traced here: 52.3 us
  Pallas kernels  46.1 us (88%)
  local copies, waits for them, and re-layouts  3.55 us (7%)
  between operations  2.58 us (5%)
    pallas_call x1, Pallas kernels, on_device(): pl.pallas_call(functools.partial(kernel, far, pairs), out_shape=(out, out...  46.1 us
    unnamed x6, local copies, waits for them, and re-layouts  3.55 us

profile of v3, /device:TPU:0, one launch (start us, length us, event | category | flops | bytes accessed | tf_op | source)
XLA Modules:
  0.0 52.3 jit_solution(16544281585433821707)
XLA Ops:
  2.6 0.0 copy-start
  2.6 1.0 %copy-done = bf16[128,1152]{1,0:T(8,128)(2,1)S(1)} copy-done((bf16[128,1152]{1,0:T(8,128)(2,1)S(1)}, bf16[128,1152]{1,0:T(8,128)(2,1)}, u32[]{:S(2)}) %copy-start) | copy-done | bytes 294936
  3.5 0.0 copy-start.1
  3.5 1.0 %copy-done.1 = bf16[128,1152]{1,0:T(8,128)(2,1)S(1)} copy-done((bf16[128,1152]{1,0:T(8,128)(2,1)S(1)}, bf16[128,1152]{1,0:T(8,128)(2,1)}, u32[]{:S(2)}) %copy-start.1) | copy-done | bytes 294936
  4.5 46.1 %shard_map.68 = (f32[128,1152]{1,0:T(8,128)S(1)}, f32[128,1152]{1,0:T(8,128)S(1)}) custom-call(bf16[128,1152]{1,0:T(8,128)(2,1)S(1)} %copy-done, bf16[128,1152]{1,0:T(8,128)(2,1)S(1)} %copy-done.1, f32[1]{0:T(128)S(6)} %copy.9.multiplier_ref, f32[1]{0:T(128)S(6)} %copy.10.offset_ref, f32[1]{0:T(128)S(6)} %copy.11.adjoint_ref), custom_call_target="tpu_custom_call" | custom-call | tf_op jit(solution)/shard_map/pallas_call | solution.py:316
  50.6 0.8 %copy.12 = f32[128,1152]{1,0:T(8,128)} copy(f32[128,1152]{1,0:T(8,128)S(1)} %get-tuple-element.4) | data formatting | bytes 1179648
  51.5 0.8 %copy.13 = f32[128,1152]{1,0:T(8,128)} copy(f32[128,1152]{1,0:T(8,128)S(1)} %get-tuple-element.5) | data formatting | bytes 1179648
Async XLA Ops:
  2.6 1.0 %copy-start = (bf16[128,1152]{1,0:T(8,128)(2,1)S(1)}, bf16[128,1152]{1,0:T(8,128)(2,1)}, u32[]{:S(2)}) copy-start(bf16[128,1152]{1,0:T(8,128)(2,1)} %picture_hbm.1) | copy-start | bytes 884740
  3.5 1.0 %copy-start.1 = (bf16[128,1152]{1,0:T(8,128)(2,1)S(1)}, bf16[128,1152]{1,0:T(8,128)(2,1)}, u32[]{:S(2)}) copy-start(bf16[128,1152]{1,0:T(8,128)(2,1)} %caption_hbm.1) | copy-start | bytes 884740

commit v4 on v3

--- a/solution.py
+++ b/solution.py
@@ -10,7 +10,7 @@
 
 MESH = pl.DeviceIdType.MESH
 CHUNKS = 4
-AHEAD = 2
+AHEAD = 4
 BF16 = jnp.bfloat16
 F32 = jnp.float32
 
@@ -236,31 +236,14 @@
             d_txt[mine, :] + recv_c[mine, :].astype(F32)
         ).astype(BF16)
 
-    for_tiles(1, far, far_tiles)
-    for k in range(AHEAD):
-        start_x(k)
-    lines, columns = pl.ds(0, tile), pl.ds(2 * tile, 2 * tile)
-    coup[lines, columns] = sigmoid_tile(lines, columns).astype(BF16)
-    core_part(1)
-    own_part(1)
-    core_part(0)
-    for c in every:
-        y_sum(1, c)
-        if c < AHEAD:
-            start_y(c)
-    image_part(0)
-    own_part(0)
-    for c in every:
-        y_sum(0, c)
-
-    for c in every:
-        start_x(c + AHEAD)
+    def forward_z(c):
         for d in range(1, far):
             grad_x[d, c].wait_recv()
             mine = pl.ds(d * rows + c * part, part)
             send_z[mine, :] = (d_img[mine, :] + recv_x[mine, :].astype(F32)).astype(BF16)
             grad_z[d, c] = send(send_z, d, recv_z, far - d, c, at_far[d])
-        start_y(c + AHEAD)
+
+    def forward_near(c):
         grad_c[1, 0, c].wait_recv()
         grad_y[1, c].wait_recv()
         mine = pl.ds(2 * rows + c * part, part)
@@ -271,9 +254,30 @@
             + recv_y[pl.ds(rows + c * part, part), :].astype(F32)
         ).astype(BF16)
         grad_w[c] = send(send_w, 0, recv_w, 0, c, at_near)
-    for k in range(CHUNKS + AHEAD, 2 * CHUNKS):
-        start_x(k)
-        start_y(k)
+
+    for_tiles(1, far, far_tiles)
+    for c in every:
+        start_x(c)
+    lines, columns = pl.ds(0, tile), pl.ds(2 * tile, 2 * tile)
+    coup[lines, columns] = sigmoid_tile(lines, columns).astype(BF16)
+    core_part(1)
+    own_part(1)
+    for c in every:
+        y_sum(1, c)
+        start_y(c)
+    image_part(0)
+    for c in range(CHUNKS // 2):
+        forward_z(c)
+        start_x(CHUNKS + c)
+    core_part(0)
+    for c in range(CHUNKS // 2, CHUNKS):
+        forward_z(c)
+        start_x(CHUNKS + c)
+    own_part(0)
+    for c in every:
+        y_sum(0, c)
+        start_y(CHUNKS + c)
+        forward_near(c)
 
     samples = rows * pairs
     derivative = adjoint_ref[0] * multiplier / samples
@@ -313,7 +317,7 @@
         return pltpu.VMEM((count * rows, width), kind)
 
     out = jax.ShapeDtypeStruct((rows, width), F32)
-    return pl.pallas_call(
+    grads = pl.pallas_call(
         functools.partial(kernel, far, pairs),
         out_shape=(out, out),
         in_specs=[hbm, hbm, smem, smem, smem],
@@ -343,7 +347,41 @@
         compiler_params=pltpu.CompilerParams(
             collective_id=0, has_side_effects=True, vmem_limit_bytes=52 * 1024 * 1024
         ),
-    )(picture, caption, multiplier, offset, adjoint)
+    )(
+        pltpu.with_memory_space_constraint(picture, pltpu.HBM),
+        pltpu.with_memory_space_constraint(caption, pltpu.HBM),
+        multiplier,
+        offset,
+        adjoint,
+    )
+    return copied_out(*grads)
+
+
+def copy_out_kernel(image_ref, text_ref, image_out, text_out, sem):
+    copies = [
+        pltpu.make_async_copy(image_ref, image_out, sem.at[0]),
+        pltpu.make_async_copy(text_ref, text_out, sem.at[1]),
+    ]
+    for copy in copies:
+        copy.start()
+    for copy in copies:
+        copy.wait()
+
+
+def copied_out(image_grad, text_grad):
+    hbm = pl.BlockSpec(memory_space=pltpu.HBM)
+    anywhere = pl.BlockSpec(memory_space=pl.ANY)
+    return pl.pallas_call(
+        copy_out_kernel,
+        out_shape=(
+            jax.ShapeDtypeStruct(image_grad.shape, F32),
+            jax.ShapeDtypeStruct(text_grad.shape, F32),
+        ),
+        in_specs=[anywhere, anywhere],
+        out_specs=(hbm, hbm),
+        scratch_shapes=[pltpu.SemaphoreType.DMA((2,))],
+        compiler_params=pltpu.CompilerParams(vmem_limit_bytes=4 * 1024 * 1024),
+    )(image_grad, text_grad)
 
 
 def solution(mesh):

time: 52.5 us -> 52.5 us (level)
  Pallas kernels: 46.1 us -> 49.8 us
  local copies, waits for them, and re-layouts: 3.55 us -> 0 us
    unnamed x6 -> x0, local copies, waits for them, and re-layouts: 3.55 us -> none
    pallas_call x1, Pallas kernels: 46.1 us -> 48.7 us  [on_device(): pl.pallas_call(functools.partial(kernel, far, pairs), out_shape=(out, out...]
    pallas_call x0 -> x1, Pallas kernels: none -> 1.03 us  [copied_out(): pl.pallas_call(copy_out_kernel, out_shape=(jax.ShapeDtypeStruct(image_gra...]
where the time goes in v4:
time: 52.5 us; the launch traced here: 52.3 us
  Pallas kernels  49.8 us (95%)
  between operations  2.57 us (5%)
    pallas_call x1, Pallas kernels, on_device(): pl.pallas_call(functools.partial(kernel, far, pairs), out_shape=(out, out...  48.7 us

profile of v4, /device:TPU:0, one launch (start us, length us, event | category | flops | bytes accessed | tf_op | source)
XLA Modules:
  0.0 52.3 jit_solution(8858051174249234960)
XLA Ops:
  2.6 48.7 %shard_map.68 = (f32[128,1152]{1,0:T(8,128)S(1)}, f32[128,1152]{1,0:T(8,128)S(1)}) custom-call(bf16[128,1152]{1,0:T(8,128)(2,1)} %picture_hbm.1, bf16[128,1152]{1,0:T(8,128)(2,1)} %caption_hbm.1, f32[1]{0:T(128)S(6)} %copy.7.multiplier_ref, f32[1]{0:T(128)S(6)} %copy.8.offset_ref, f32[1]{0:T(128)S(6)} %copy.9.adjoint_ref), custom_call_target="tpu_custom_call" | custom-call | tf_op jit(solution)/shard_map/pallas_call | solution.py:320
  51.3 1.0 %shard_map.69 = (f32[128,1152]{1,0:T(8,128)}, f32[128,1152]{1,0:T(8,128)}) custom-call(f32[128,1152]{1,0:T(8,128)S(1)} %get-tuple-element.4.image_ref, f32[128,1152]{1,0:T(8,128)S(1)} %get-tuple-element.5.text_ref), custom_call_target="tpu_custom_call" | custom-call | tf_op jit(solution)/shard_map/pallas_call | solution.py:374

commit v5 on v4

--- a/solution.py
+++ b/solution.py
@@ -9,8 +9,9 @@
 from jax.sharding import PartitionSpec as P
 
 MESH = pl.DeviceIdType.MESH
-CHUNKS = 4
-AHEAD = 4
+CHUNKS = 8
+AHEAD = 8
+Z_AHEAD = 2
 BF16 = jnp.bfloat16
 F32 = jnp.float32
 
@@ -124,14 +125,15 @@
 
     def start_z(c):
         for d in range(1, far):
-            if c > 0:
-                sent(img_z[d, c - 1])
+            if c >= Z_AHEAD:
+                sent(img_z[d, c - Z_AHEAD])
             img_z[d, c] = send(img, 0, img, 2 * (far - d), c, at_far[d])
-        if c > 0:
-            sent(txt_z[c - 1])
+        if c >= Z_AHEAD:
+            sent(txt_z[c - Z_AHEAD])
         txt_z[c] = send(txt, 0, txt, 4, c, at_near)
 
-    start_z(0)
+    for c in range(Z_AHEAD):
+        start_z(c)
     for c in every:
         img_x[0, c] = send(img, 0, img, 1, c, at_x)
         txt_y[0, c] = send(txt, 0, txt, 1, c, at_y)
@@ -157,8 +159,8 @@
         coup[lines, columns] = (values - jnp.where(same, 1.0, 0.0)).astype(BF16)
 
     for c in every:
-        if c + 1 < CHUNKS:
-            start_z(c + 1)
+        if c + Z_AHEAD < CHUNKS:
+            start_z(c + Z_AHEAD)
         for d in range(1, far):
             img_z[d, c].wait_recv()
             img_x[d, c] = send(img, 2 * (far - d), img, 2 * (far - d) + 1, c, at_x)

time: 52.5 us -> 55 us (1.048)
  Pallas kernels: 49.8 us -> 52.2 us
    pallas_call x1, Pallas kernels: 48.7 us -> 51.2 us  [on_device(): pl.pallas_call(functools.partial(kernel, far, pairs), out_shape=(out, out...]
where the time goes in v5:
time: 55 us; the launch traced here: 54.8 us
  Pallas kernels  52.2 us (95%)
  between operations  2.57 us (5%)
    pallas_call x1, Pallas kernels, on_device(): pl.pallas_call(functools.partial(kernel, far, pairs), out_shape=(out, out...  51.2 us

profile of v5, /device:TPU:0, one launch (start us, length us, event | category | flops | bytes accessed | tf_op | source)
XLA Modules:
  0.0 54.8 jit_solution(17566377747735925595)
XLA Ops:
  2.6 51.2 %shard_map.68 = (f32[128,1152]{1,0:T(8,128)S(1)}, f32[128,1152]{1,0:T(8,128)S(1)}) custom-call(bf16[128,1152]{1,0:T(8,128)(2,1)} %picture_hbm.1, bf16[128,1152]{1,0:T(8,128)(2,1)} %caption_hbm.1, f32[1]{0:T(128)S(6)} %copy.7.multiplier_ref, f32[1]{0:T(128)S(6)} %copy.8.offset_ref, f32[1]{0:T(128)S(6)} %copy.9.adjoint_ref), custom_call_target="tpu_custom_call" | custom-call | tf_op jit(solution)/shard_map/pallas_call | solution.py:322
  53.8 1.0 %shard_map.69 = (f32[128,1152]{1,0:T(8,128)}, f32[128,1152]{1,0:T(8,128)}) custom-call(f32[128,1152]{1,0:T(8,128)S(1)} %get-tuple-element.4.image_ref, f32[128,1152]{1,0:T(8,128)S(1)} %get-tuple-element.5.text_ref), custom_call_target="tpu_custom_call" | custom-call | tf_op jit(solution)/shard_map/pallas_call | solution.py:376

commit v6 on v5

--- a/solution.py
+++ b/solution.py
@@ -9,8 +9,8 @@
 from jax.sharding import PartitionSpec as P
 
 MESH = pl.DeviceIdType.MESH
-CHUNKS = 8
-AHEAD = 8
+CHUNKS = 2
+AHEAD = 2
 Z_AHEAD = 2
 BF16 = jnp.bfloat16
 F32 = jnp.float32

time: 55 us -> 51 us (0.927)
  Pallas kernels: 52.2 us -> 48.3 us
    pallas_call x1, Pallas kernels: 51.2 us -> 47.2 us  [on_device(): pl.pallas_call(functools.partial(kernel, far, pairs), out_shape=(out, out...]
where the time goes in v6:
time: 51 us; the launch traced here: 50.8 us
  Pallas kernels  48.3 us (95%)
  between operations  2.57 us (5%)
    pallas_call x1, Pallas kernels, on_device(): pl.pallas_call(functools.partial(kernel, far, pairs), out_shape=(out, out...  47.2 us
    pallas_call x1, Pallas kernels, copied_out(): pl.pallas_call(copy_out_kernel, out_shape=(jax.ShapeDtypeStruct(image_gra...  1.03 us

profile of v6, /device:TPU:0, one launch (start us, length us, event | category | flops | bytes accessed | tf_op | source)
XLA Modules:
  0.0 50.8 jit_solution(17997917590140920172)
XLA Ops:
  2.6 47.2 %shard_map.68 = (f32[128,1152]{1,0:T(8,128)S(1)}, f32[128,1152]{1,0:T(8,128)S(1)}) custom-call(bf16[128,1152]{1,0:T(8,128)(2,1)} %picture_hbm.1, bf16[128,1152]{1,0:T(8,128)(2,1)} %caption_hbm.1, f32[1]{0:T(128)S(6)} %copy.7.multiplier_ref, f32[1]{0:T(128)S(6)} %copy.8.offset_ref, f32[1]{0:T(128)S(6)} %copy.9.adjoint_ref), custom_call_target="tpu_custom_call" | custom-call | tf_op jit(solution)/shard_map/pallas_call | solution.py:322
  49.8 1.0 %shard_map.69 = (f32[128,1152]{1,0:T(8,128)}, f32[128,1152]{1,0:T(8,128)}) custom-call(f32[128,1152]{1,0:T(8,128)S(1)} %get-tuple-element.4.image_ref, f32[128,1152]{1,0:T(8,128)S(1)} %get-tuple-element.5.text_ref), custom_call_target="tpu_custom_call" | custom-call | tf_op jit(solution)/shard_map/pallas_call | solution.py:376

commit v7 on v6

--- a/solution.py
+++ b/solution.py
@@ -11,7 +11,7 @@
 MESH = pl.DeviceIdType.MESH
 CHUNKS = 2
 AHEAD = 2
-Z_AHEAD = 2
+Z_AHEAD = 1
 BF16 = jnp.bfloat16
 F32 = jnp.float32
 
@@ -92,19 +92,14 @@
     for peer in [at_x, at_near, at_y, at_core] + at_far[1:]:
         pl.semaphore_signal(barrier, inc=1, device_id=peer, device_id_type=MESH)
 
-    load_picture.wait()
-    img[pl.ds(0, rows), :] = unit_rows(picture_ref[...])[0].astype(BF16)
-    load_caption.wait()
-    txt[pl.ds(0, rows), :] = unit_rows(caption_ref[...])[0].astype(BF16)
-    pl.semaphore_wait(barrier, 3 + far)
-
     started = {}
 
     def send(src, src_slot, dst, dst_slot, chunk, peer):
         number = len(started)
+        first, length = (0, rows) if chunk is None else (chunk * part, part)
         copy = pltpu.make_async_remote_copy(
-            src_ref=src.at[pl.ds(src_slot * rows + chunk * part, part), :],
-            dst_ref=dst.at[pl.ds(dst_slot * rows + chunk * part, part), :],
+            src_ref=src.at[pl.ds(src_slot * rows + first, length), :],
+            dst_ref=dst.at[pl.ds(dst_slot * rows + first, length), :],
             send_sem=send_sem.at[number],
             recv_sem=recv_sem.at[number],
             device_id=peer,
@@ -123,22 +118,31 @@
     every = range(CHUNKS)
     img_z, txt_z, img_x, txt_y, txt_c = {}, {}, {}, {}, {}
 
-    def start_z(c):
+    def start_img_z(c):
         for d in range(1, far):
             if c >= Z_AHEAD:
                 sent(img_z[d, c - Z_AHEAD])
             img_z[d, c] = send(img, 0, img, 2 * (far - d), c, at_far[d])
+
+    def start_txt_z(c):
         if c >= Z_AHEAD:
             sent(txt_z[c - Z_AHEAD])
         txt_z[c] = send(txt, 0, txt, 4, c, at_near)
 
+    load_picture.wait()
+    img[pl.ds(0, rows), :] = unit_rows(picture_ref[...])[0].astype(BF16)
+    pl.semaphore_wait(barrier, 3 + far)
     for c in range(Z_AHEAD):
-        start_z(c)
+        start_img_z(c)
     for c in every:
         img_x[0, c] = send(img, 0, img, 1, c, at_x)
+    load_caption.wait()
+    txt[pl.ds(0, rows), :] = unit_rows(caption_ref[...])[0].astype(BF16)
+    for c in range(Z_AHEAD):
+        start_txt_z(c)
+    for c in every:
         txt_y[0, c] = send(txt, 0, txt, 1, c, at_y)
-    for c in every:
-        txt_c[0, c] = send(txt, 0, txt, 2, c, at_core)
+    txt_c[0] = send(txt, 0, txt, 2, None, at_core)
 
     multiplier, offset = multiplier_ref[0], offset_ref[0]
     tile = 2 * rows
@@ -159,23 +163,25 @@
         coup[lines, columns] = (values - jnp.where(same, 1.0, 0.0)).astype(BF16)
 
     for c in every:
-        if c + Z_AHEAD < CHUNKS:
-            start_z(c + Z_AHEAD)
         for d in range(1, far):
             img_z[d, c].wait_recv()
             img_x[d, c] = send(img, 2 * (far - d), img, 2 * (far - d) + 1, c, at_x)
+        if c + Z_AHEAD < CHUNKS:
+            start_img_z(c + Z_AHEAD)
         txt_z[c].wait_recv()
         txt_y[1, c] = send(txt, 4, txt, 5, c, at_y)
+        if c + Z_AHEAD < CHUNKS:
+            start_txt_z(c + Z_AHEAD)
         txt_c[2, c] = send(txt, 4, txt, 6, c, at_core)
-        if c == CHUNKS // 2:
+        if c == 0:
             for e in every:
                 txt_y[0, e].wait_recv()
-                txt_c[1, e] = send(txt, 1, txt, 3, e, at_core)
-    for c in every:
-        img_x[0, c].wait_recv()
-        txt_c[0, c].wait_recv()
-        txt_c[1, c].wait_recv()
-    near_tiles()
+            txt_c[1] = send(txt, 1, txt, 3, None, at_core)
+            for e in every:
+                img_x[0, e].wait_recv()
+            txt_c[0].wait_recv()
+            txt_c[1].wait_recv()
+            near_tiles()
     for c in every:
         txt_y[1, c].wait_recv()
         txt_c[3, c] = send(txt, 5, txt, 7, c, at_core)

time: 51 us -> 54.7 us (1.073)
  Pallas kernels: 48.3 us -> 51.9 us
    pallas_call x1, Pallas kernels: 47.2 us -> 50.9 us  [on_device(): pl.pallas_call(functools.partial(kernel, far, pairs), out_shape=(out, out...]
where the time goes in v7:
time: 54.7 us; the launch traced here: 54.5 us
  Pallas kernels  51.9 us (95%)
  between operations  2.57 us (5%)
    pallas_call x1, Pallas kernels, on_device(): pl.pallas_call(functools.partial(kernel, far, pairs), out_shape=(out, out...  50.9 us

profile of v7, /device:TPU:0, one launch (start us, length us, event | category | flops | bytes accessed | tf_op | source)
XLA Modules:
  0.0 54.5 jit_solution(14701342250080037336)
XLA Ops:
  2.6 50.9 %shard_map.68 = (f32[128,1152]{1,0:T(8,128)S(1)}, f32[128,1152]{1,0:T(8,128)S(1)}) custom-call(bf16[128,1152]{1,0:T(8,128)(2,1)} %picture_hbm.1, bf16[128,1152]{1,0:T(8,128)(2,1)} %caption_hbm.1, f32[1]{0:T(128)S(6)} %copy.7.multiplier_ref, f32[1]{0:T(128)S(6)} %copy.8.offset_ref, f32[1]{0:T(128)S(6)} %copy.9.adjoint_ref), custom_call_target="tpu_custom_call" | custom-call | tf_op jit(solution)/shard_map/pallas_call | solution.py:328
  53.5 1.0 %shard_map.69 = (f32[128,1152]{1,0:T(8,128)}, f32[128,1152]{1,0:T(8,128)}) custom-call(f32[128,1152]{1,0:T(8,128)S(1)} %get-tuple-element.4.image_ref, f32[128,1152]{1,0:T(8,128)S(1)} %get-tuple-element.5.text_ref), custom_call_target="tpu_custom_call" | custom-call | tf_op jit(solution)/shard_map/pallas_call | solution.py:382

commit v8 on v7

--- a/solution.py
+++ b/solution.py
@@ -11,7 +11,6 @@
 MESH = pl.DeviceIdType.MESH
 CHUNKS = 2
 AHEAD = 2
-Z_AHEAD = 1
 BF16 = jnp.bfloat16
 F32 = jnp.float32
 
@@ -118,29 +117,17 @@
     every = range(CHUNKS)
     img_z, txt_z, img_x, txt_y, txt_c = {}, {}, {}, {}, {}
 
-    def start_img_z(c):
-        for d in range(1, far):
-            if c >= Z_AHEAD:
-                sent(img_z[d, c - Z_AHEAD])
-            img_z[d, c] = send(img, 0, img, 2 * (far - d), c, at_far[d])
-
-    def start_txt_z(c):
-        if c >= Z_AHEAD:
-            sent(txt_z[c - Z_AHEAD])
-        txt_z[c] = send(txt, 0, txt, 4, c, at_near)
-
     load_picture.wait()
     img[pl.ds(0, rows), :] = unit_rows(picture_ref[...])[0].astype(BF16)
     pl.semaphore_wait(barrier, 3 + far)
-    for c in range(Z_AHEAD):
-        start_img_z(c)
-    for c in every:
+    for c in every:
+        for d in range(1, far):
+            img_z[d, c] = send(img, 0, img, 2 * (far - d), c, at_far[d])
         img_x[0, c] = send(img, 0, img, 1, c, at_x)
     load_caption.wait()
     txt[pl.ds(0, rows), :] = unit_rows(caption_ref[...])[0].astype(BF16)
-    for c in range(Z_AHEAD):
-        start_txt_z(c)
-    for c in every:
+    for c in every:
+        txt_z[c] = send(txt, 0, txt, 4, c, at_near)
         txt_y[0, c] = send(txt, 0, txt, 1, c, at_y)
     txt_c[0] = send(txt, 0, txt, 2, None, at_core)
 
@@ -163,32 +150,35 @@
         coup[lines, columns] = (values - jnp.where(same, 1.0, 0.0)).astype(BF16)
 
     for c in every:
+        txt_y[0, c].wait_recv()
+    txt_c[1] = send(txt, 1, txt, 3, None, at_core)
+    for c in every:
+        img_x[0, c].wait_recv()
+    txt_c[0].wait_recv()
+    txt_c[1].wait_recv()
+    near_tiles()
+    for c in every:
         for d in range(1, far):
             img_z[d, c].wait_recv()
             img_x[d, c] = send(img, 2 * (far - d), img, 2 * (far - d) + 1, c, at_x)
-        if c + Z_AHEAD < CHUNKS:
-            start_img_z(c + Z_AHEAD)
         txt_z[c].wait_recv()
         txt_y[1, c] = send(txt, 4, txt, 5, c, at_y)
-        if c + Z_AHEAD < CHUNKS:
-            start_txt_z(c + Z_AHEAD)
-        txt_c[2, c] = send(txt, 4, txt, 6, c, at_core)
-        if c == 0:
-            for e in every:
-                txt_y[0, e].wait_recv()
-            txt_c[1] = send(txt, 1, txt, 3, None, at_core)
-            for e in every:
-                img_x[0, e].wait_recv()
-            txt_c[0].wait_recv()
-            txt_c[1].wait_recv()
-            near_tiles()
+    txt_c[2] = send(txt, 4, txt, 6, None, at_core)
     for c in every:
         txt_y[1, c].wait_recv()
         txt_c[3, c] = send(txt, 5, txt, 7, c, at_core)
     for c in every:
         for d in range(1, far):
             img_x[d, c].wait_recv()
-        txt_c[2, c].wait_recv()
+
+    def far_near_tiles(step):
+        lines = pl.ds(pl.multiple_of(step * tile, tile), tile)
+        columns = pl.ds(0, 2 * tile)
+        coup[lines, columns] = sigmoid_tile(lines, columns).astype(BF16)
+
+    for_tiles(1, far, far_near_tiles)
+    txt_c[2].wait_recv()
+    for c in every:
         txt_c[3, c].wait_recv()
 
     def image_part(step):
@@ -200,7 +190,8 @@
 
     def far_tiles(step):
         lines = pl.ds(pl.multiple_of(step * tile, tile), tile)
-        coup[lines, :] = sigmoid_tile(lines, slice(None)).astype(BF16)
+        columns = pl.ds(2 * tile, 2 * tile)
+        coup[lines, columns] = sigmoid_tile(lines, columns).astype(BF16)
         image_part(step)
 
     def text_part(slot):
@@ -231,14 +222,14 @@
     def core_part(dz):
         send_c[pl.ds(2 * dz * rows, tile), :] = text_part(dz * 4 + 2).astype(BF16)
         for dy in (1, 0):
-            for c in every:
-                grad_c[dz, dy, c] = send(send_c, dz * 2 + dy, recv_c, dz * 2 + dy, c, at_core)
+            grad_c[dz, dy] = send(send_c, dz * 2 + dy, recv_c, dz * 2 + dy, None, at_core)
 
     def own_part(dz):
         d_txt[pl.ds(2 * dz * rows, tile), :] = text_part(dz * 4)
 
     def y_sum(dz, c):
-        grad_c[dz, 1, c].wait_recv()
+        if c == 0:
+            grad_c[dz, 1].wait_recv()
         mine = pl.ds((2 * dz + 1) * rows + c * part, part)
         send_y[pl.ds(dz * rows + c * part, part), :] = (
             d_txt[mine, :] + recv_c[mine, :].astype(F32)
@@ -252,7 +243,8 @@
             grad_z[d, c] = send(send_z, d, recv_z, far - d, c, at_far[d])
 
     def forward_near(c):
-        grad_c[1, 0, c].wait_recv()
+        if c == 0:
+            grad_c[1, 0].wait_recv()
         grad_y[1, c].wait_recv()
         mine = pl.ds(2 * rows + c * part, part)
         here = pl.ds(c * part, part)
@@ -298,7 +290,8 @@
             total += recv_z[pl.ds((far - d) * rows + c * part, part), :].astype(F32)
         unit, scale = unit_rows(picture_ref[here, :])
         image_grad_ref[here, :] = unit_grad(unit, scale, derivative * total)
-        grad_c[0, 0, c].wait_recv()
+        if c == 0:
+            grad_c[0, 0].wait_recv()
         grad_y[0, c].wait_recv()
         grad_w[c].wait_recv()
         total = (

time: 54.7 us -> 54.3 us (level)
  no operation moved by 1% of the time
where the time goes in v8:
time: 54.3 us; the launch traced here: 54.1 us
  Pallas kernels  51.6 us (95%)
  between operations  2.57 us (5%)
    pallas_call x1, Pallas kernels, on_device(): pl.pallas_call(functools.partial(kernel, far, pairs), out_shape=(out, out...  50.5 us

profile of v8, /device:TPU:0, one launch (start us, length us, event | category | flops | bytes accessed | tf_op | source)
XLA Modules:
  0.0 54.1 jit_solution(2294035373505631225)
XLA Ops:
  2.6 50.5 %shard_map.68 = (f32[128,1152]{1,0:T(8,128)S(1)}, f32[128,1152]{1,0:T(8,128)S(1)}) custom-call(bf16[128,1152]{1,0:T(8,128)(2,1)} %picture_hbm.1, bf16[128,1152]{1,0:T(8,128)(2,1)} %caption_hbm.1, f32[1]{0:T(128)S(6)} %copy.7.multiplier_ref, f32[1]{0:T(128)S(6)} %copy.8.offset_ref, f32[1]{0:T(128)S(6)} %copy.9.adjoint_ref), custom_call_target="tpu_custom_call" | custom-call | tf_op jit(solution)/shard_map/pallas_call | solution.py:321
  53.1 1.0 %shard_map.69 = (f32[128,1152]{1,0:T(8,128)}, f32[128,1152]{1,0:T(8,128)}) custom-call(f32[128,1152]{1,0:T(8,128)S(1)} %get-tuple-element.4.image_ref, f32[128,1152]{1,0:T(8,128)S(1)} %get-tuple-element.5.text_ref), custom_call_target="tpu_custom_call" | custom-call | tf_op jit(solution)/shard_map/pallas_call | solution.py:375

commit v9 on v6

--- a/solution.py
+++ b/solution.py
@@ -172,16 +172,24 @@
                 txt_y[0, e].wait_recv()
                 txt_c[1, e] = send(txt, 1, txt, 3, e, at_core)
     for c in every:
+        txt_y[1, c].wait_recv()
+        txt_c[3, c] = send(txt, 5, txt, 7, c, at_core)
+    for c in every:
         img_x[0, c].wait_recv()
         txt_c[0, c].wait_recv()
         txt_c[1, c].wait_recv()
     near_tiles()
     for c in every:
-        txt_y[1, c].wait_recv()
-        txt_c[3, c] = send(txt, 5, txt, 7, c, at_core)
-    for c in every:
         for d in range(1, far):
             img_x[d, c].wait_recv()
+
+    def far_near_tiles(step):
+        lines = pl.ds(pl.multiple_of(step * tile, tile), tile)
+        columns = pl.ds(0, 2 * tile)
+        coup[lines, columns] = sigmoid_tile(lines, columns).astype(BF16)
+
+    for_tiles(1, far, far_near_tiles)
+    for c in every:
         txt_c[2, c].wait_recv()
         txt_c[3, c].wait_recv()
 
@@ -194,7 +202,8 @@
 
     def far_tiles(step):
         lines = pl.ds(pl.multiple_of(step * tile, tile), tile)
-        coup[lines, :] = sigmoid_tile(lines, slice(None)).astype(BF16)
+        columns = pl.ds(2 * tile, 2 * tile)
+        coup[lines, columns] = sigmoid_tile(lines, columns).astype(BF16)
         image_part(step)
 
     def text_part(slot):

time: 51 us -> 52.2 us (1.024)
  Pallas kernels: 48.3 us -> 49.5 us
    pallas_call x1, Pallas kernels: 47.2 us -> 48.4 us  [on_device(): pl.pallas_call(functools.partial(kernel, far, pairs), out_shape=(out, out...]
where the time goes in v9:
time: 52.2 us; the launch traced here: 52 us
  Pallas kernels  49.5 us (95%)
  between operations  2.57 us (5%)
    pallas_call x1, Pallas kernels, on_device(): pl.pallas_call(functools.partial(kernel, far, pairs), out_shape=(out, out...  48.4 us

profile of v9, /device:TPU:0, one launch (start us, length us, event | category | flops | bytes accessed | tf_op | source)
XLA Modules:
  0.0 52.0 jit_solution(5750478000940753538)
XLA Ops:
  2.6 48.4 %shard_map.68 = (f32[128,1152]{1,0:T(8,128)S(1)}, f32[128,1152]{1,0:T(8,128)S(1)}) custom-call(bf16[128,1152]{1,0:T(8,128)(2,1)} %picture_hbm.1, bf16[128,1152]{1,0:T(8,128)(2,1)} %caption_hbm.1, f32[1]{0:T(128)S(6)} %copy.7.multiplier_ref, f32[1]{0:T(128)S(6)} %copy.8.offset_ref, f32[1]{0:T(128)S(6)} %copy.9.adjoint_ref), custom_call_target="tpu_custom_call" | custom-call | tf_op jit(solution)/shard_map/pallas_call | solution.py:331
  51.0 1.0 %shard_map.69 = (f32[128,1152]{1,0:T(8,128)}, f32[128,1152]{1,0:T(8,128)}) custom-call(f32[128,1152]{1,0:T(8,128)S(1)} %get-tuple-element.4.image_ref, f32[128,1152]{1,0:T(8,128)S(1)} %get-tuple-element.5.text_ref), custom_call_target="tpu_custom_call" | custom-call | tf_op jit(solution)/shard_map/pallas_call | solution.py:385

commit v10 on v6

--- a/solution.py
+++ b/solution.py
@@ -9,9 +9,9 @@
 from jax.sharding import PartitionSpec as P
 
 MESH = pl.DeviceIdType.MESH
-CHUNKS = 2
-AHEAD = 2
-Z_AHEAD = 2
+CHUNKS = 4
+AHEAD = 4
+Z_AHEAD = 4
 BF16 = jnp.bfloat16
 F32 = jnp.float32
 

time: 51 us -> 52.9 us (1.037)
  Pallas kernels: 48.3 us -> 50.1 us
    pallas_call x1, Pallas kernels: 47.2 us -> 49.1 us  [on_device(): pl.pallas_call(functools.partial(kernel, far, pairs), out_shape=(out, out...]
where the time goes in v10:
time: 52.9 us; the launch traced here: 52.7 us
  Pallas kernels  50.1 us (95%)
  between operations  2.57 us (5%)
    pallas_call x1, Pallas kernels, on_device(): pl.pallas_call(functools.partial(kernel, far, pairs), out_shape=(out, out...  49.1 us

profile of v10, /device:TPU:0, one launch (start us, length us, event | category | flops | bytes accessed | tf_op | source)
XLA Modules:
  0.0 52.7 jit_solution(10242386706231164466)
XLA Ops:
  2.6 49.1 %shard_map.68 = (f32[128,1152]{1,0:T(8,128)S(1)}, f32[128,1152]{1,0:T(8,128)S(1)}) custom-call(bf16[128,1152]{1,0:T(8,128)(2,1)} %picture_hbm.1, bf16[128,1152]{1,0:T(8,128)(2,1)} %caption_hbm.1, f32[1]{0:T(128)S(6)} %copy.7.multiplier_ref, f32[1]{0:T(128)S(6)} %copy.8.offset_ref, f32[1]{0:T(128)S(6)} %copy.9.adjoint_ref), custom_call_target="tpu_custom_call" | custom-call | tf_op jit(solution)/shard_map/pallas_call | solution.py:322
  51.7 1.0 %shard_map.69 = (f32[128,1152]{1,0:T(8,128)}, f32[128,1152]{1,0:T(8,128)}) custom-call(f32[128,1152]{1,0:T(8,128)S(1)} %get-tuple-element.4.image_ref, f32[128,1152]{1,0:T(8,128)S(1)} %get-tuple-element.5.text_ref), custom_call_target="tpu_custom_call" | custom-call | tf_op jit(solution)/shard_map/pallas_call | solution.py:376
